TPU v7x, 32 devices: a whole 2x2x4 slice. The times are simulated.
32 devices in a mesh: grp: 2 (over y), row: 4 (over z), col: 4 (over x, core).
Axes of the slice: x: 2, y: 2, z: 4, core: 2. Of those that a mesh axis runs over, the one named last changes fastest.
Arguments:
- train_in: bfloat16 [18432, 4096], P(('grp', 'row'), 'col'), parts along dimension 0, may hold values from -6 to 6
- train_grad: bfloat16 [18432, 4096], P(('grp', 'row'), 'col'), parts along dimension 0, may hold values from -6 to 6
- query_in: bfloat16 [3072, 4096], P(('grp', 'row'), 'col'), parts along dimension 0, may hold values from -6 to 6
- query_grad: bfloat16 [3072, 4096], P(('grp', 'row'), 'col'), parts along dimension 0, may hold values from -6 to 6
- proj_in: bfloat16 [4096, 128], P('col'), may hold values from -0.09375 to 0.09375
- proj_out: bfloat16 [4096, 128], P('col'), may hold values from -0.09375 to 0.09375
- inv_fisher: bfloat16 [16384, 16384], P('row', 'col'), may hold values from -0.046875 to 0.046875
- train_len: int32 [384], P(('grp', 'row')), parts along dimension 0, may hold values from 8 to 48, as said below
- query_len: int32 [64], P(('grp', 'row')), parts along dimension 0, may hold values from 8 to 48, as said below
Outputs:
- scores: float32 [32, 384], P(None, ('grp', 'row', 'col')), parts along dimension 1
There are 2 independent parts, one for each index of `grp`. A program takes and returns all parts, laid end to end along the dimension named above; an argument that names none is the same for every part. Nothing has to cross between parts.
Inputs may be any that keep to these rules, and one draw needn't show every extreme that they name: `train_len`: live tokens come first in a cell. Some cell in every draw has all 48 slots live and some has the fewest allowed. `query_len`: live tokens come first in a cell. Some cell in every draw has all 48 slots live and some has the fewest allowed.
All inputs are finite; a program needn't handle non-finite values.
Results may differ from a plain program's by a relative error of at most 0.04.
Values may be sent and summed in bfloat16 or wider, within the bound.
A program may use at most 128 MiB of HBM per device.

v0:
```python
import jax
import jax.numpy as jnp
from jax import lax
from jax.sharding import PartitionSpec as P

CELL = 48


def live_weights(lengths):
    position = lax.broadcasted_iota(jnp.int32, (lengths.shape[0], CELL), 1)
    scale = 1.0 / lengths[:, None].astype(jnp.float32)
    weight = jnp.where(position < lengths[:, None], scale, jnp.zeros_like(scale))
    return weight.reshape(-1, 1)


def outer_sums(back, acts, count):
    back_cells = back.reshape(count, CELL, back.shape[1])
    acts_cells = acts.reshape(count, CELL, acts.shape[1])
    gram = jnp.einsum("eta,etb->eab", back_cells, acts_cells, preferred_element_type=jnp.float32)
    return gram.reshape(count, -1).astype(jnp.bfloat16)


def body(
    train_in, train_grad, query_in, query_grad, proj_in, proj_out, inv_fisher, train_len, query_len
):
    col_count = lax.axis_size("col")
    row_count = lax.axis_size("row")
    col_index = lax.axis_index("col")
    rank_size = proj_in.shape[1]
    owned = train_len.shape[0] // col_count
    band = rank_size // col_count
    query_acts = jnp.dot(query_in, proj_in, preferred_element_type=jnp.float32).astype(jnp.bfloat16)
    query_back = jnp.dot(query_grad, proj_out, preferred_element_type=jnp.float32).astype(
        jnp.bfloat16
    )
    query_acts_sum, query_back_sum = (
        lax.psum(query_acts, "col").astype(jnp.float32),
        lax.psum(query_back, "col").astype(jnp.float32),
    )
    query_weight = live_weights(query_len)
    back_band = lax.dynamic_slice_in_dim(query_back_sum, col_index * band, band, 1)
    back_band_w = (back_band * query_weight).astype(jnp.bfloat16)
    query_block = outer_sums(back_band_w, query_acts_sum.astype(jnp.bfloat16), query_len.shape[0])
    pre_part = lax.dot_general(
        lax.all_gather(query_block, "row", axis=0, tiled=True),
        inv_fisher,
        (((1,), (1,)), ((), ())),
        preferred_element_type=jnp.float32,
    )
    shares = lax.psum_scatter(pre_part.astype(jnp.bfloat16), "col", scatter_dimension=1, tiled=True)
    pre_rows = lax.all_gather(shares, "col", axis=1, tiled=True)
    train_acts = jnp.dot(train_in, proj_in, preferred_element_type=jnp.float32).astype(jnp.bfloat16)
    train_back = jnp.dot(train_grad, proj_out, preferred_element_type=jnp.float32).astype(
        jnp.bfloat16
    )
    owned_rows = owned * CELL
    acts_full, back_full = (
        lax.psum(train_acts, "col").astype(jnp.float32),
        lax.psum(train_back, "col").astype(jnp.float32),
    )
    acts_sum = lax.dynamic_slice_in_dim(acts_full, col_index * owned_rows, owned_rows, 0)
    back_sum = lax.dynamic_slice_in_dim(back_full, col_index * owned_rows, owned_rows, 0)
    owned_len = lax.dynamic_slice_in_dim(train_len, col_index * owned, owned, 0)
    back_weighted = (back_sum * live_weights(owned_len)).astype(jnp.bfloat16)
    grads = outer_sums(back_weighted, acts_sum.astype(jnp.bfloat16), owned)
    grad_blocks = grads.reshape(owned, row_count, grads.shape[1] // row_count)
    partial_value = jnp.einsum(
        "qk,ejk->qje",
        pre_rows,
        lax.all_to_all(grad_blocks, "row", split_axis=1, concat_axis=1, tiled=True),
        preferred_element_type=jnp.float32,
    )
    totals = lax.psum(partial_value, "row")
    mine = lax.dynamic_slice_in_dim(totals, lax.axis_index("row"), 1, 1)
    return mine.reshape(totals.shape[0], owned)


def solution(mesh):
    in_specs = (
        P(("grp", "row"), "col"),
        P(("grp", "row"), "col"),
        P(("grp", "row"), "col"),
        P(("grp", "row"), "col"),
        P("col", None),
        P("col", None),
        P("row", "col"),
        P(("grp", "row")),
        P(("grp", "row")),
    )
    out_specs = P(None, ("grp", "row", "col"))
    return jax.shard_map(body, mesh=mesh, in_specs=in_specs, out_specs=out_specs, check_vma=False)
```

profile of v0, /device:TPU:0, one launch (start us, length us, event | category | flops | bytes accessed | tf_op | source)
XLA Modules:
  0.0 144.2 jit_solution(6744412709842028275)
XLA Ops:
  6.5 0.0 copy-start
  6.5 0.0 copy-start.2
  6.5 0.0 copy-start.3
  6.5 0.0 all-reduce.3.cloned.1.call-start
  6.5 0.0 copy-start.6
  6.6 4.7 %convolution_convert_fusion.1 = bf16[2304,128]{1,0:T(8,128)(2,1)} fusion(bf16[2304,1024]{1,0:T(8,128)(2,1)} %param.9, bf16[1024,128]{1,0:T(8,128)(2,1)} %param.13), kind=kOutput, calls=%fused_computation.1 | convolution fusion | flops 604274688 | bytes 5570560 | tf_op jit(solution)/shard_map/dot_general | solution.py:52
  11.3 0.0 copy-done
  11.3 0.0 copy-done.2
  11.3 0.0 copy-start.1
  11.3 1.0 convolution_convert_fusion.4
  12.3 0.0 copy-done.3
  12.3 0.0 copy-done.6
  12.3 0.0 copy-start.5
  12.3 0.0 copy-start.4
  12.3 2.2 %convolution_convert_fusion.2 = bf16[2304,128]{1,0:T(8,128)(2,1)} fusion(bf16[2304,1024]{1,0:T(8,128)(2,1)S(1)} %copy-done.6, bf16[1024,128]{1,0:T(8,128)(2,1)S(1)} %copy-done.3), kind=kOutput, calls=%fused_computation.2 | convolution fusion | flops 604274688 | bytes 5570560 | tf_op jit(solution)/shard_map/dot_general | solution.py:53
  14.5 0.0 copy-done.1
  14.5 1.0 convolution_convert_fusion.5
  15.6 0.0 all-reduce.3.cloned.1.call-update
  15.6 0.0 reduce-scatter.2.cloned.1.call-start
  15.7 0.0 copy-done.5
  15.7 0.1 convert_divide_fusion.1
  15.8 0.1 fusion.3
  15.8 0.1 select_n.38
  15.9 0.0 copy-done.4
  15.9 0.1 fusion.4
  16.0 0.1 select_n.41
  16.1 42.8 %all-reduce.3.cloned.1.call-done = (bf16[2304,128]{1,0:T(8,128)(2,1)}, bf16[2304,128]{1,0:T(8,128)(2,1)}, bf16[8,48,128]{2,1,0:T(8,128)(2,1)}, bf16[384,128]{0,1:T(8,128)(2,1)}) async-done(((bf16[2304,128]{1,0:T(8,128)(2,1)}, bf16[2304,128]{1,0:T(8,128)(2,1)}, bf16[8,48,128]{2,1,0:T(8,128)(2,1)}, bf16[384,128]{0,1:T(8,128)(2,1)}), (bf16[2304,128]{1,0:T(8,128)(2,1)}, bf16[2304,128]{1,0:T(8,128)(2,1)}, ...) | async-done | bytes 1376272 | tf_op jit(solution)/shard_map/psum | solution.py:59
  58.9 0.7 multiply_convert_fusion.1
  59.6 0.1 reshape.81
  59.7 1.0 fusion
  60.8 13.9 %all_gather.6 = bf16[32,4096]{1,0:T(8,128)(2,1)S(1)} all-gather(bf16[8,4096]{1,0:T(8,128)(2,1)S(1)} %bitcast.34), channel_id=1, replica_groups=mesh['grp'=2,'row'=4,'col'=4] {'row'}, dimensions={0}, use_global_device_ids=true | all-gather | bytes 327680 | tf_op jit(solution)/shard_map/all_gather | solution.py:45
  74.7 16.0 %convolution_convert_fusion = bf16[32,4096]{1,0:T(8,128)(2,1)} fusion(bf16[32,4096]{1,0:T(8,128)(2,1)S(1)} %all_gather.6, bf16[4096,4096]{1,0:T(8,128)(2,1)} %param.15), kind=kOutput, calls=%fused_computation | convolution fusion | flops 1073872896 | bytes 34078720 | tf_op jit(solution)/shard_map/dot_general | solution.py:44
  90.7 0.0 reduce-scatter.2.cloned.1.call-update
  90.7 0.9 convert_convert_fusion
  91.6 1.1 multiply_convert_fusion
  92.7 0.3 convolution_convert_fusion.3
  93.0 0.1 convert_element_type.64
  93.1 1.0 copy.10
  94.1 5.2 %all-to-all-start = ((bf16[12,4,4096]{2,0,1:T(8,128)(2,1)}), bf16[12,4,4096]{2,0,1:T(8,128)(2,1)S(1)}, u32[]{:S(2)}, u32[]{:S(2)}) async-start(bf16[12,4,4096]{2,0,1:T(8,128)(2,1)} %copy.10), calls=%async_computation | async-start | bytes 1048576 | tf_op jit(solution)/shard_map/all_to_all | solution.py:70
  99.4 12.1 %reduce-scatter.2.cloned.1.call-done = bf16[32,1024]{1,0:T(8,128)(2,1)} async-done(((bf16[32,4096]{1,0:T(8,128)(2,1)}), bf16[32,1024]{1,0:T(8,128)(2,1)}) %reduce-scatter.2.cloned.1.call-update) | async-done | bytes 65552 | tf_op jit(solution)/shard_map/reduce_scatter | solution.py:50
  111.5 6.0 %all_gather.7 = bf16[32,4096]{1,0:T(8,128)(2,1)S(1)} all-gather(bf16[32,1024]{1,0:T(8,128)(2,1)} %reduce-scatter.2.cloned.1.call-done), channel_id=1, replica_groups=mesh['grp'=2,'row'=4,'col'=4] {'col'}, dimensions={1}, use_global_device_ids=true | all-gather | bytes 327680 | tf_op jit(solution)/shard_map/all_gather | solution.py:51
  117.5 0.0 all-to-all-done
  117.5 0.3 convolution_bitcast_fusion
  117.8 19.0 %psum.39 = f32[32,4,12]{0,2,1:T(8,128)S(1)} all-reduce(f32[32,4,12]{0,2,1:T(8,128)S(1)} %convolution_bitcast_fusion), channel_id=1, replica_groups=mesh['grp'=2,'row'=4,'col'=4] {'row'}, use_global_device_ids=true, to_apply=%region_5.6 | all-reduce | flops 1536 | bytes 12288 | tf_op jit(solution)/shard_map/psum | solution.py:73
  136.8 0.6 dynamic-slice_bitcast_fusion
  (2 shorter events, 0.0 us)
Async XLA Ops:
  6.5 4.7 %copy-start = (bf16[384,1024]{1,0:T(8,128)(2,1)S(1)}, bf16[384,1024]{1,0:T(8,128)(2,1)}, u32[]{:S(2)}) copy-start(bf16[384,1024]{1,0:T(8,128)(2,1)} %param.11) | copy-start | bytes 2359300
  6.5 4.7 %copy-start.2 = (bf16[1024,128]{1,0:T(8,128)(2,1)S(1)}, bf16[1024,128]{1,0:T(8,128)(2,1)}, u32[]{:S(2)}) copy-start(bf16[1024,128]{1,0:T(8,128)(2,1)} %param.13) | copy-start | bytes 786436
  6.5 5.8 %copy-start.3 = (bf16[1024,128]{1,0:T(8,128)(2,1)S(1)}, bf16[1024,128]{1,0:T(8,128)(2,1)}, u32[]{:S(2)}) copy-start(bf16[1024,128]{1,0:T(8,128)(2,1)} %param.14) | copy-start | bytes 786436
  6.5 52.3 %all-reduce.3.cloned.1.call-start = ((), (), s32[]{:S(2)}) async-start(), calls=%async_computation.3 | async-start | bytes 2752512 | tf_op jit(solution)/shard_map/psum | solution.py:59
  6.5 5.8 %copy-start.6 = (bf16[2304,1024]{1,0:T(8,128)(2,1)S(1)}, bf16[2304,1024]{1,0:T(8,128)(2,1)}, u32[]{:S(2)}) copy-start(bf16[2304,1024]{1,0:T(8,128)(2,1)} %param.10) | copy-start | bytes 14155780
  11.3 3.3 %copy-start.1 = (bf16[384,1024]{1,0:T(8,128)(2,1)S(1)}, bf16[384,1024]{1,0:T(8,128)(2,1)}, u32[]{:S(2)}) copy-start(bf16[384,1024]{1,0:T(8,128)(2,1)} %param.12) | copy-start | bytes 2359300
  12.3 3.4 %copy-start.5 = (s32[48]{0:T(128)S(1)}, s32[48]{0:T(128)}, u32[]{:S(2)}) copy-start(s32[48]{0:T(128)} %param.16) | copy-start | bytes 580
  12.3 3.6 %copy-start.4 = (s32[8]{0:T(128)S(1)}, s32[8]{0:T(128)}, u32[]{:S(2)}) copy-start(s32[8]{0:T(128)} %param.17) | copy-start | bytes 100
  15.6 95.9 %reduce-scatter.2.cloned.1.call-start = ((), (), s32[]{:S(2)}) async-start(), calls=%async_computation.2 | async-start | bytes 327680 | tf_op jit(solution)/shard_map/reduce_scatter | solution.py:50
  94.1 23.4 %all-to-all-start = ((bf16[12,4,4096]{2,0,1:T(8,128)(2,1)}), bf16[12,4,4096]{2,0,1:T(8,128)(2,1)S(1)}, u32[]{:S(2)}, u32[]{:S(2)}) async-start(bf16[12,4,4096]{2,0,1:T(8,128)(2,1)} %copy.10), calls=%async_computation | async-start | bytes 1048576 | tf_op jit(solution)/shard_map/all_to_all | solution.py:70
Sparse Core Ops, SparseCore 0:
  15.7 43.1 all-reduce.2
  90.8 20.6 reduce-scatter.1
where the time goes:
time: 145 us; the launch traced here: 144 us
  waiting for transfers between devices  55 us (38%)
  blocking collectives  38.9 us (27%)
  matrix products  26.6 us (18%)
  between operations  13.5 us (9%)
  starting transfers between devices  5.28 us (4%)
  other arithmetic  2.96 us (2%)
  local copies, waits for them, and re-layouts  2.05 us (1%)
    psum x1, waiting for transfers between devices, body(): lax.psum(train_back, 'col').astype(jnp.float32)  42.8 us
    psum x1, blocking collectives, body(): totals = lax.psum(partial_value, 'row')  19 us
    dot_general x1, matrix products, body(): lax.dot_general(lax.all_gather(query_block, 'row', axis=0, tiled=True), i...  16 us
    all_gather x1, blocking collectives, body(): lax.all_gather(query_block, 'row', axis=0, tiled=True)  13.9 us
    reduce_scatter x1, waiting for transfers between devices, body(): lax.psum_scatter(pre_part.astype(jnp.bfloat16), 'col', scatter_dimension=...  12.1 us
    all_gather x1, blocking collectives, body(): pre_rows = lax.all_gather(shares, 'col', axis=1, tiled=True)  5.98 us
    all_to_all x1, starting transfers between devices, body(): lax.all_to_all(grad_blocks, 'row', split_axis=1, concat_axis=1, tiled=True)  5.24 us
    dot_general x1, matrix products, body(): jnp.dot(train_in, proj_in, preferred_element_type=jnp.float32)  4.72 us
  transfers between devices with their start and end apart: 3, of which 2 were waited for; matrix products, arithmetic and copies ran while one was open for 3% of the time, Pallas kernels for 0%

commit v1 on v0

v1 whole, which is shorter than its diff:
```python
import functools

import jax
import jax.numpy as jnp
from jax import lax
from jax.experimental import pallas as pl
from jax.experimental.pallas import tpu as pltpu
from jax.sharding import PartitionSpec as P

CELL = 48
F32 = jnp.float32
BF16 = jnp.bfloat16
MESH = pl.DeviceIdType.MESH


def token_weights(lens, base, count):
    tok = lax.broadcasted_iota(jnp.int32, (1, count * CELL), 1)
    length = jnp.ones_like(tok)
    start = jnp.zeros_like(tok)
    for e in range(count):
        here = tok >= e * CELL
        length = jnp.where(here, lens[base + e], length)
        start = jnp.where(here, e * CELL, start)
    scale = 1.0 / length.astype(F32)
    return jnp.where(tok - start < length, scale, jnp.zeros_like(scale))


def kernel(
    R, C,
    train_in, train_grad, query_in, query_grad, proj_in, proj_out, fisher, train_len, query_len,
    out,
    tin, tgr, qin, qgr, pin, pout, fbuf,
    qa_send, qa_recv, qb_send, qb_recv, gath, gt,
    t_send, t_recv, bw, g_send, g_recv, p_send, p_recv, s_send, s_recv,
    lsem, tsem, fsem, qas, qar, qbs, qbr, gs, gr, ts, tr, ggs, ggr, ps, pr, ss, sr,
):
    r = lax.axis_index("row")
    c = lax.axis_index("col")
    N = R * C
    QT, RANK = qa_send.shape
    QC = QT // CELL
    OT = tin.shape[1]
    owned = OT // CELL
    band = qb_send.shape[1]
    Q = R * QC
    KC = fbuf.shape[1]
    ka = bw.shape[1]
    kb = KC // ka

    def row_at(i):
        return lax.rem(r + i, R)

    def col_at(i):
        return lax.rem(c + i, C)

    def remote(src, dst, send, recv, rr, cc):
        return pltpu.make_async_remote_copy(
            src_ref=src, dst_ref=dst, send_sem=send, recv_sem=recv,
            device_id={"row": rr, "col": cc}, device_id_type=MESH,
        )

    def peer(n):
        return lax.rem(r + n // C, R), lax.rem(c + n % C, C)

    def back_peer(n):
        return lax.rem(r + R - n // C, R), lax.rem(c + C - n % C, C)

    loads = [
        pltpu.make_async_copy(a, b, lsem.at[i])
        for i, (a, b) in enumerate(
            [(query_in, qin), (proj_in, pin), (query_grad, qgr), (proj_out, pout)]
        )
    ]
    for load in loads:
        load.start()

    barrier = pltpu.get_barrier_semaphore()

    @pl.loop(1, N)
    def _(n):
        rr, cc = peer(n)
        pl.semaphore_signal(barrier, inc=1, device_id={"row": rr, "col": cc}, device_id_type=MESH)

    order = list(range(1, C)) + [0]
    tloads = {}
    for i in order:
        rows = pl.ds(pl.multiple_of(col_at(i) * OT, 16), OT)
        tloads[i] = (
            pltpu.make_async_copy(train_in.at[rows], tin.at[i], tsem.at[0, i]),
            pltpu.make_async_copy(train_grad.at[rows], tgr.at[i], tsem.at[1, i]),
        )
        tloads[i][0].start()
        tloads[i][1].start()

    loads[0].wait()
    loads[1].wait()
    qa_send[...] = jnp.dot(qin[...], pin[...], preferred_element_type=F32).astype(BF16)
    pl.semaphore_wait(barrier, N - 1)
    qa = [None] + [
        remote(qa_send, qa_recv.at[i], qas.at[i], qar.at[i], r, col_at(i)) for i in range(1, C)
    ]
    for i in range(1, C):
        qa[i].start()
    loads[2].wait()
    loads[3].wait()
    back = jnp.dot(qgr[...], pout[...], preferred_element_type=F32)
    back_t = back.T.astype(BF16)
    for i in range(C):
        qb_send[i] = back_t[i * band:(i + 1) * band]
    qb = [None] + [
        remote(qb_send.at[col_at(i)], qb_recv.at[i], qbs.at[i], qbr.at[i], r, col_at(i))
        for i in range(1, C)
    ]
    for i in range(1, C):
        qb[i].start()

    floads = {}
    for i in order:
        rows = pl.ds(pl.multiple_of(col_at(i) * KC, 16), KC)
        floads[i] = pltpu.make_async_copy(fisher.at[rows], fbuf.at[i], fsem.at[i])
        floads[i].start()

    tc = {}
    for i in order:
        tloads[i][0].wait()
        t_send[i, 0] = jnp.dot(tin[i], pin[...], preferred_element_type=F32).astype(BF16)
        tloads[i][1].wait()
        t_send[i, 1] = jnp.dot(tgr[i], pout[...], preferred_element_type=F32).astype(BF16)
        if i:
            tc[i] = remote(t_send.at[i], t_recv.at[i], ts.at[i], tr.at[i], r, col_at(i))
            tc[i].start()

    acts = qa_send[...].astype(F32)
    for i in range(1, C):
        qa[i].wait_recv()
        acts = acts + qa_recv[i].astype(F32)
    backs = qb_send[c].astype(F32)
    for i in range(1, C):
        qb[i].wait_recv()
        backs = backs + qb_recv[i].astype(F32)
    backs = (backs * token_weights(query_len, 0, QC)).astype(BF16)
    pick = lax.broadcasted_iota(jnp.int32, (band, QC, band), 0) == lax.broadcasted_iota(
        jnp.int32, (band, QC, band), 2
    )
    pick = jnp.where(pick, 1.0, 0.0).reshape(band * QC, band).astype(BF16)
    spread = jnp.dot(pick, backs, preferred_element_type=F32).reshape(band, QC, QT)
    first = lax.broadcasted_iota(jnp.int32, (band, QC, QT), 1) * CELL
    tok = lax.broadcasted_iota(jnp.int32, (band, QC, QT), 2)
    spread = jnp.where((tok >= first) & (tok < first + CELL), spread, 0.0)
    gath[r] = jnp.dot(
        spread.reshape(band * QC, QT).astype(BF16), acts.astype(BF16), preferred_element_type=F32
    ).astype(BF16)
    gc = [None] + [
        remote(gath.at[r], gath.at[r], gs.at[i], gr.at[i], row_at(i), c) for i in range(1, R)
    ]
    for i in range(1, R):
        gc[i].start()

    t_acts = t_send[0, 0].astype(F32)
    t_back = t_send[0, 1].astype(F32)
    for i in range(1, C):
        tc[i].wait_recv()
        t_acts = t_acts + t_recv[i, 0].astype(F32)
        t_back = t_back + t_recv[i, 1].astype(F32)
    t_acts = t_acts.astype(BF16)
    weight = token_weights(train_len, c * owned, owned)
    t_back = (t_back.T * weight).astype(BF16).astype(F32)
    halves = RANK // kb
    for n in range(N):
        a0 = n * KC // RANK
        bw[n] = t_back[a0:a0 + ka]
    first = lax.broadcasted_iota(jnp.int32, (owned, ka, OT), 0) * CELL
    tok = lax.broadcasted_iota(jnp.int32, (owned, ka, OT), 2)
    live = (tok >= first) & (tok < first + CELL)

    def grads_for(chunk):
        lhs = jnp.where(live, bw[chunk][None], 0.0).reshape(owned * ka, OT).astype(BF16)
        both = jnp.dot(lhs, t_acts, preferred_element_type=F32)
        if halves == 1:
            return both.astype(BF16)
        value = both[:, :kb]
        for h in range(1, halves):
            value = jnp.where(lax.rem(chunk, halves) == h, both[:, h * kb:(h + 1) * kb], value)
        return value.astype(BF16)

    def grads_copy(n):
        rr, cc = peer(n)
        return remote(g_send.at[n], g_recv.at[n], ggs.at[n], ggr.at[n], rr, cc)

    g_recv[0] = grads_for(r * C + c)

    @pl.loop(1, N)
    def _(n):
        rr, cc = peer(n)
        g_send[n] = grads_for(rr * C + cc)
        grads_copy(n).start()

    for i in range(1, R):
        here = lax.rem(r + R - i, R)
        remote(gath.at[here], gath.at[here], gs.at[i], gr.at[i], row_at(i), c).wait_recv()
    whole = gath[...].astype(F32)
    for a in range(band):
        rows = [whole[i, a * QC:(a + 1) * QC] for i in range(R)]
        gt[a * RANK:(a + 1) * RANK] = jnp.concatenate(rows, 0).T.astype(BF16)

    pc = {}
    for i in order:
        floads[i].wait()
        part = jnp.dot(fbuf[i], gt[...], preferred_element_type=F32).astype(BF16)
        for a in range(ka):
            p_send[i, :, a * Q:(a + 1) * Q] = part[a * kb:(a + 1) * kb]
        if i:
            pc[i] = remote(p_send.at[i], p_recv.at[i], ps.at[i], pr.at[i], r, col_at(i))
            pc[i].start()
    pre = p_send[0].astype(F32)
    for i in range(1, C):
        pc[i].wait_recv()
        pre = pre + p_recv[i].astype(F32)
    pre = pre.astype(BF16)

    @pl.loop(1, N)
    def _(n):
        grads_copy(n).wait_recv()

    lhs = g_recv[...].reshape(N * owned * ka, kb)
    every = jnp.dot(lhs, pre, preferred_element_type=F32).reshape(N, owned, ka, ka * Q)
    lane = lax.broadcasted_iota(jnp.int32, (N, owned, ka, ka * Q), 3)
    low = lax.broadcasted_iota(jnp.int32, (N, owned, ka, ka * Q), 2) * Q
    every = jnp.sum(jnp.where((lane >= low) & (lane < low + Q), every, 0.0), axis=2)
    value = every[:, :, :Q]
    for a in range(1, ka):
        value = value + every[:, :, a * Q:(a + 1) * Q]
    s_send[...] = value

    def score_copy(n):
        rr, cc = back_peer(n)
        return remote(s_send.at[n], s_recv.at[n], ss.at[n], sr.at[n], rr, cc)

    @pl.loop(1, N)
    def _(n):
        score_copy(n).start()

    @pl.loop(1, N)
    def _(n):
        score_copy(n).wait_recv()

    s_recv[0] = s_send[0]
    out[...] = jnp.sum(s_recv[...], axis=0)

    for i in range(1, C):
        qa[i].wait_send()
        qb[i].wait_send()
        tc[i].wait_send()
        pc[i].wait_send()
    for i in range(1, R):
        gc[i].wait_send()

    @pl.loop(1, N)
    def _(n):
        grads_copy(n).wait_send()
        score_copy(n).wait_send()


def body(R, C, *args):
    train_in, train_grad, query_in, query_grad, proj_in, proj_out, fisher, train_len, query_len = args
    T, D = train_in.shape
    QT = query_in.shape[0]
    rank = proj_in.shape[1]
    K1, J = fisher.shape
    N = R * C
    OT = T // C
    owned = OT // CELL
    QC = QT // CELL
    Q = R * QC
    band = rank // C
    KC = K1 // C
    ka = max(1, KC // rank)
    kb = KC // ka
    dma = pltpu.SemaphoreType.DMA
    scratch = [
        pltpu.VMEM((C, OT, D), BF16),
        pltpu.VMEM((C, OT, D), BF16),
        pltpu.VMEM((QT, D), BF16),
        pltpu.VMEM((QT, D), BF16),
        pltpu.VMEM((D, rank), BF16),
        pltpu.VMEM((D, rank), BF16),
        pltpu.VMEM((C, KC, J), BF16),
        pltpu.VMEM((QT, rank), BF16),
        pltpu.VMEM((C, QT, rank), BF16),
        pltpu.VMEM((C, band, QT), BF16),
        pltpu.VMEM((C, band, QT), BF16),
        pltpu.VMEM((R, band * QC, rank), BF16),
        pltpu.VMEM((J, Q), BF16),
        pltpu.VMEM((C, 2, OT, rank), BF16),
        pltpu.VMEM((C, 2, OT, rank), BF16),
        pltpu.VMEM((N, ka, OT), F32),
        pltpu.VMEM((N, owned * ka, kb), BF16),
        pltpu.VMEM((N, owned * ka, kb), BF16),
        pltpu.VMEM((C, kb, ka * Q), BF16),
        pltpu.VMEM((C, kb, ka * Q), BF16),
        pltpu.VMEM((N, owned, Q), F32),
        pltpu.VMEM((N, owned, Q), F32),
        dma((4,)), dma((2, C)), dma((C,)),
        dma((C,)), dma((C,)), dma((C,)), dma((C,)),
        dma((R,)), dma((R,)),
        dma((C,)), dma((C,)),
        dma((N,)), dma((N,)),
        dma((C,)), dma((C,)),
        dma((N,)), dma((N,)),
    ]
    flops = 2 * rank * D * 2 * (T + QT) + 2 * Q * K1 * J
    scores = pl.pallas_call(
        functools.partial(kernel, R, C),
        out_shape=jax.ShapeDtypeStruct((owned, Q), F32),
        in_specs=[pl.BlockSpec(memory_space=pl.ANY)] * 7
        + [pl.BlockSpec(memory_space=pltpu.SMEM)] * 2,
        out_specs=pl.BlockSpec(memory_space=pltpu.VMEM),
        scratch_shapes=scratch,
        compiler_params=pltpu.CompilerParams(
            collective_id=0, has_side_effects=True, vmem_limit_bytes=60 * 2**20
        ),
        cost_estimate=pl.CostEstimate(
            flops=flops, bytes_accessed=2 * (K1 * J + 2 * D * (T + QT + rank)), transcendentals=0
        ),
    )(*args)
    return scores.T


def solution(mesh):
    cells = P(("grp", "row"))
    data = P(("grp", "row"), "col")
    proj = P("col", None)
    in_specs = (data, data, data, data, proj, proj, P("row", "col"), cells, cells)
    run = functools.partial(body, mesh.shape["row"], mesh.shape["col"])
    return jax.shard_map(
        run, mesh=mesh, in_specs=in_specs, out_specs=P(None, ("grp", "row", "col")), check_vma=False
    )
```

time: 145 us -> 56.7 us (0.39)
  Pallas kernels: 0 us -> 55.2 us
  waiting for transfers between devices: 55 us -> 0 us
  blocking collectives: 38.9 us -> 0 us
  matrix products: 26.6 us -> 0 us
  between operations: 13.5 us -> 0.01 us
  starting transfers between devices: 5.28 us -> 0 us
  other arithmetic: 2.96 us -> 0 us
    pallas_call x0 -> x1, Pallas kernels: none -> 55.2 us  [body(): pl.pallas_call(functools.partial(kernel, R, C), out_shape=jax.ShapeDtypeS...]
    psum x1 -> x0, waiting for transfers between devices: 42.8 us -> none  [body(): lax.psum(train_back, 'col').astype(jnp.float32)]
    dot_general x8 -> x0, matrix products: 26.6 us -> none  [the longest x1 16 us: body(): lax.dot_general(lax.all_gather(query_block, 'row', axis=0, tiled=True), i...]
    all_gather x2 -> x0, blocking collectives: 19.9 us -> none  [the longest x1 13.9 us: body(): lax.all_gather(query_block, 'row', axis=0, tiled=True)]
    psum x1 -> x0, blocking collectives: 19 us -> none  [body(): totals = lax.psum(partial_value, 'row')]
    reduce_scatter x1 -> x0, waiting for transfers between devices: 12.1 us -> none  [body(): lax.psum_scatter(pre_part.astype(jnp.bfloat16), 'col', scatter_dimension=...]
    all_to_all x1 -> x0, starting transfers between devices: 5.24 us -> none  [body(): lax.all_to_all(grad_blocks, 'row', split_axis=1, concat_axis=1, tiled=True)]
    convert_element_type x3 -> x0, other arithmetic: 2.73 us -> none  [the longest x1 1.06 us: body(): back_weighted = (back_sum * live_weights(owned_len)).astype(jnp.bfloat16)]
  transfers between devices with their start and end apart: 3 -> 0, of which waited for: 2 -> 0; matrix products, arithmetic and copies ran while one was open for 3% -> 0% of each run, Pallas kernels for 0% -> 0%
where the time goes in v1:
time: 56.7 us; the launch traced here: 56.5 us
  Pallas kernels  55.2 us (97%)
  local copies, waits for them, and re-layouts  1.3 us (2%)
    pallas_call x1, Pallas kernels, body(): pl.pallas_call(functools.partial(kernel, R, C), out_shape=jax.ShapeDtypeS...  55.2 us
    unnamed x1, local copies, waits for them, and re-layouts  1.3 us

profile of v1, /device:TPU:0, one launch (start us, length us, event | category | flops | bytes accessed | tf_op | source)
XLA Modules:
  0.0 56.5 jit_solution(16366998300598742720)
XLA Ops:
  0.0 55.2 %shard_map.91 = f32[12,32]{1,0:T(8,128)} custom-call(bf16[2304,1024]{1,0:T(8,128)(2,1)} %train_in.1, bf16[2304,1024]{1,0:T(8,128)(2,1)} %train_grad.1, bf16[384,1024]{1,0:T(8,128)(2,1)} %query_in.1, bf16[384,1024]{1,0:T(8,128)(2,1)} %query_grad.1, bf16[1024,128]{1,0:T(8,128)(2,1)} %proj_in.1, bf16[1024,128]{1,0:T(8,128)(2,1)} %proj_out.1, ...), custom_call_target="tpu_custom_call" | custom-call | flops 2483027968 | bytes 45088768 | tf_op jit(solution)/shard_map/pallas_call | solution.py:312
  55.2 1.3 %copy.11 = f32[32,12]{0,1:T(8,128)} copy(f32[32,12]{0,1:T(8,128)} %bitcast.1) | data formatting | bytes 3072

commit v2 on v1

--- a/solution.py
+++ b/solution.py
@@ -11,6 +11,15 @@
 F32 = jnp.float32
 BF16 = jnp.bfloat16
 MESH = pl.DeviceIdType.MESH
+
+
+def dot2(a, b):
+    half = a.shape[0] // 32 * 16
+    if half == 0:
+        return jnp.dot(a, b, preferred_element_type=F32)
+    top = jnp.dot(a[:half], b, preferred_element_type=F32)
+    low = jnp.dot(a[half:], b, preferred_element_type=F32)
+    return jnp.concatenate([top, low], 0)
 
 
 def token_weights(lens, base, count):
@@ -26,13 +35,13 @@
 
 
 def kernel(
-    R, C,
+    R, C, G,
     train_in, train_grad, query_in, query_grad, proj_in, proj_out, fisher, train_len, query_len,
     out,
     tin, tgr, qin, qgr, pin, pout, fbuf,
     qa_send, qa_recv, qb_send, qb_recv, gath, gt,
-    t_send, t_recv, bw, g_send, g_recv, p_send, p_recv, s_send, s_recv,
-    lsem, tsem, fsem, qas, qar, qbs, qbr, gs, gr, ts, tr, ggs, ggr, ps, pr, ss, sr,
+    t_send, t1_recv, t2_recv, bw, g_send, g_recv, p_send, p_recv, s_send, s_recv,
+    lsem, tsem, fsem, qas, qar, qbs, qbr, gs, gr, ts, t1r, t2r, ggs, ggr, ps, pr, ss, sr,
 ):
     r = lax.axis_index("row")
     c = lax.axis_index("col")
@@ -82,9 +91,14 @@
         pl.semaphore_signal(barrier, inc=1, device_id={"row": rr, "col": cc}, device_id_type=MESH)
 
     order = list(range(1, C)) + [0]
+    X = C // G
+    torder = [(j, s) for s in range(G) for j in list(range(1, X)) + [0]]
+    chip, core = c // G, lax.rem(c, G)
     tloads = {}
-    for i in order:
-        rows = pl.ds(pl.multiple_of(col_at(i) * OT, 16), OT)
+    for j, s in torder:
+        i = s * X + j
+        owner = lax.rem(chip + j, X) * G + lax.rem(core + 1 + s, G)
+        rows = pl.ds(pl.multiple_of(owner * OT, 16), OT)
         tloads[i] = (
             pltpu.make_async_copy(train_in.at[rows], tin.at[i], tsem.at[0, i]),
             pltpu.make_async_copy(train_grad.at[rows], tgr.at[i], tsem.at[1, i]),
@@ -94,7 +108,7 @@
 
     loads[0].wait()
     loads[1].wait()
-    qa_send[...] = jnp.dot(qin[...], pin[...], preferred_element_type=F32).astype(BF16)
+    qa_send[...] = dot2(qin[...], pin[...]).astype(BF16)
     pl.semaphore_wait(barrier, N - 1)
     qa = [None] + [
         remote(qa_send, qa_recv.at[i], qas.at[i], qar.at[i], r, col_at(i)) for i in range(1, C)
@@ -103,7 +117,7 @@
         qa[i].start()
     loads[2].wait()
     loads[3].wait()
-    back = jnp.dot(qgr[...], pout[...], preferred_element_type=F32)
+    back = dot2(qgr[...], pout[...])
     back_t = back.T.astype(BF16)
     for i in range(C):
         qb_send[i] = back_t[i * band:(i + 1) * band]
@@ -120,15 +134,33 @@
         floads[i] = pltpu.make_async_copy(fisher.at[rows], fbuf.at[i], fsem.at[i])
         floads[i].start()
 
-    tc = {}
-    for i in order:
+    t1 = {}
+    t2 = {}
+    mate = chip * G + lax.rem(core + 1, G)
+    for j, s in torder:
+        i = s * X + j
         tloads[i][0].wait()
-        t_send[i, 0] = jnp.dot(tin[i], pin[...], preferred_element_type=F32).astype(BF16)
+        left = dot2(tin[i], pin[...])
         tloads[i][1].wait()
-        t_send[i, 1] = jnp.dot(tgr[i], pout[...], preferred_element_type=F32).astype(BF16)
-        if i:
-            tc[i] = remote(t_send.at[i], t_recv.at[i], ts.at[i], tr.at[i], r, col_at(i))
-            tc[i].start()
+        right = dot2(tgr[i], pout[...])
+        if s < G - 1:
+            t_send[i, 0] = left.astype(BF16)
+            t_send[i, 1] = right.astype(BF16)
+            t1[j] = remote(t_send.at[i], t1_recv.at[j], ts.at[i], t1r.at[j], r, mate)
+            t1[j].start()
+            continue
+        t_send[i, 0] = left.astype(BF16)
+        t_send[i, 1] = right.astype(BF16)
+    for j in list(range(1, X)) + [0]:
+        i = (G - 1) * X + j
+        if G > 1:
+            t1[j].wait_recv()
+            if j:
+                t_send[i] = (t_send[i].astype(F32) + t1_recv[j].astype(F32)).astype(BF16)
+        if j:
+            far = lax.rem(chip + j, X) * G + core
+            t2[j] = remote(t_send.at[i], t2_recv.at[j], ts.at[i], t2r.at[j], r, far)
+            t2[j].start()
 
     acts = qa_send[...].astype(F32)
     for i in range(1, C):
@@ -156,12 +188,37 @@
     for i in range(1, R):
         gc[i].start()
 
-    t_acts = t_send[0, 0].astype(F32)
-    t_back = t_send[0, 1].astype(F32)
-    for i in range(1, C):
-        tc[i].wait_recv()
-        t_acts = t_acts + t_recv[i, 0].astype(F32)
-        t_back = t_back + t_recv[i, 1].astype(F32)
+    for i in range(1, R):
+        here = lax.rem(r + R - i, R)
+        remote(gath.at[here], gath.at[here], gs.at[i], gr.at[i], row_at(i), c).wait_recv()
+    whole = gath[...].astype(F32)
+    for a in range(band):
+        rows = [whole[i, a * QC:(a + 1) * QC] for i in range(R)]
+        gt[a * RANK:(a + 1) * RANK] = jnp.concatenate(rows, 0).T.astype(BF16)
+
+    pc = {}
+
+    def fisher_chunk(i):
+        floads[i].wait()
+        part = dot2(fbuf[i], gt[...]).astype(BF16)
+        for a in range(ka):
+            p_send[i, :, a * Q:(a + 1) * Q] = part[a * kb:(a + 1) * kb]
+        if i:
+            pc[i] = remote(p_send.at[i], p_recv.at[i], ps.at[i], pr.at[i], r, col_at(i))
+            pc[i].start()
+
+    early = max(1, C // 4)
+    for i in order[:early]:
+        fisher_chunk(i)
+
+    own = (G - 1) * X
+    t_sum = t_send[own].astype(F32)
+    if G > 1:
+        t_sum = t_sum + t1_recv[0].astype(F32)
+    for j in range(1, X):
+        t2[j].wait_recv()
+        t_sum = t_sum + t2_recv[j].astype(F32)
+    t_acts, t_back = t_sum[0], t_sum[1]
     t_acts = t_acts.astype(BF16)
     weight = token_weights(train_len, c * owned, owned)
     t_back = (t_back.T * weight).astype(BF16).astype(F32)
@@ -187,31 +244,29 @@
         rr, cc = peer(n)
         return remote(g_send.at[n], g_recv.at[n], ggs.at[n], ggr.at[n], rr, cc)
 
-    g_recv[0] = grads_for(r * C + c)
-
-    @pl.loop(1, N)
-    def _(n):
+    U = 4 if N % 4 == 0 else 1
+    values = []
+    for n in range(U):
         rr, cc = peer(n)
-        g_send[n] = grads_for(rr * C + cc)
+        values.append(grads_for(rr * C + cc))
+    g_recv[0] = values[0]
+    for n in range(1, U):
+        g_send[n] = values[n]
         grads_copy(n).start()
 
-    for i in range(1, R):
-        here = lax.rem(r + R - i, R)
-        remote(gath.at[here], gath.at[here], gs.at[i], gr.at[i], row_at(i), c).wait_recv()
-    whole = gath[...].astype(F32)
-    for a in range(band):
-        rows = [whole[i, a * QC:(a + 1) * QC] for i in range(R)]
-        gt[a * RANK:(a + 1) * RANK] = jnp.concatenate(rows, 0).T.astype(BF16)
-
-    pc = {}
-    for i in order:
-        floads[i].wait()
-        part = jnp.dot(fbuf[i], gt[...], preferred_element_type=F32).astype(BF16)
-        for a in range(ka):
-            p_send[i, :, a * Q:(a + 1) * Q] = part[a * kb:(a + 1) * kb]
-        if i:
-            pc[i] = remote(p_send.at[i], p_recv.at[i], ps.at[i], pr.at[i], r, col_at(i))
-            pc[i].start()
+    @pl.loop(1, N // U)
+    def _(m):
+        values = []
+        for u in range(U):
+            rr, cc = peer(m * U + u)
+            values.append(grads_for(rr * C + cc))
+        for u in range(U):
+            g_send[m * U + u] = values[u]
+        for u in range(U):
+            grads_copy(m * U + u).start()
+
+    for i in order[early:]:
+        fisher_chunk(i)
     pre = p_send[0].astype(F32)
     for i in range(1, C):
         pc[i].wait_recv()
@@ -250,8 +305,9 @@
     for i in range(1, C):
         qa[i].wait_send()
         qb[i].wait_send()
-        tc[i].wait_send()
         pc[i].wait_send()
+    for copy in list(t1.values()) + list(t2.values()):
+        copy.wait_send()
     for i in range(1, R):
         gc[i].wait_send()
 
@@ -268,6 +324,7 @@
     rank = proj_in.shape[1]
     K1, J = fisher.shape
     N = R * C
+    G = 2 if C % 2 == 0 else 1
     OT = T // C
     owned = OT // CELL
     QC = QT // CELL
@@ -292,7 +349,8 @@
         pltpu.VMEM((R, band * QC, rank), BF16),
         pltpu.VMEM((J, Q), BF16),
         pltpu.VMEM((C, 2, OT, rank), BF16),
-        pltpu.VMEM((C, 2, OT, rank), BF16),
+        pltpu.VMEM((C // G, 2, OT, rank), BF16),
+        pltpu.VMEM((C // G, 2, OT, rank), BF16),
         pltpu.VMEM((N, ka, OT), F32),
         pltpu.VMEM((N, owned * ka, kb), BF16),
         pltpu.VMEM((N, owned * ka, kb), BF16),
@@ -303,14 +361,14 @@
         dma((4,)), dma((2, C)), dma((C,)),
         dma((C,)), dma((C,)), dma((C,)), dma((C,)),
         dma((R,)), dma((R,)),
-        dma((C,)), dma((C,)),
+        dma((C,)), dma((C // G,)), dma((C // G,)),
         dma((N,)), dma((N,)),
         dma((C,)), dma((C,)),
         dma((N,)), dma((N,)),
     ]
     flops = 2 * rank * D * 2 * (T + QT) + 2 * Q * K1 * J
     scores = pl.pallas_call(
-        functools.partial(kernel, R, C),
+        functools.partial(kernel, R, C, G),
         out_shape=jax.ShapeDtypeStruct((owned, Q), F32),
         in_specs=[pl.BlockSpec(memory_space=pl.ANY)] * 7
         + [pl.BlockSpec(memory_space=pltpu.SMEM)] * 2,

time: 56.7 us -> 45.3 us (0.80)
  Pallas kernels: 55.2 us -> 43.7 us
    pallas_call x1, Pallas kernels: 55.2 us -> 43.7 us  [body(): pl.pallas_call(functools.partial(kernel, R, C, G), out_shape=jax.ShapeDty...]
where the time goes in v2:
time: 45.3 us; the launch traced here: 45 us
  Pallas kernels  43.7 us (96%)
  local copies, waits for them, and re-layouts  1.3 us (3%)
    pallas_call x1, Pallas kernels, body(): pl.pallas_call(functools.partial(kernel, R, C, G), out_shape=jax.ShapeDty...  43.7 us
    unnamed x1, local copies, waits for them, and re-layouts  1.3 us

profile of v2, /device:TPU:0, one launch (start us, length us, event | category | flops | bytes accessed | tf_op | source)
XLA Modules:
  0.0 45.0 jit_solution(14631330132601192001)
XLA Ops:
  0.0 43.7 %shard_map.91 = f32[12,32]{1,0:T(8,128)} custom-call(bf16[2304,1024]{1,0:T(8,128)(2,1)} %train_in.1, bf16[2304,1024]{1,0:T(8,128)(2,1)} %train_grad.1, bf16[384,1024]{1,0:T(8,128)(2,1)} %query_in.1, bf16[384,1024]{1,0:T(8,128)(2,1)} %query_grad.1, bf16[1024,128]{1,0:T(8,128)(2,1)} %proj_in.1, bf16[1024,128]{1,0:T(8,128)(2,1)} %proj_out.1, ...), custom_call_target="tpu_custom_call" | custom-call | flops 2483027968 | bytes 45088768 | tf_op jit(solution)/shard_map/pallas_call | solution.py:370
  43.8 1.3 %copy.11 = f32[32,12]{0,1:T(8,128)} copy(f32[32,12]{0,1:T(8,128)} %bitcast.1) | data formatting | bytes 3072
